TPU v7x, 32 devices: a whole 2x2x4 slice. The times are simulated.
32 devices in a mesh: wide: 16 (over z, x, core), narrow: 2 (over y).
Axes of the slice: x: 2, y: 2, z: 4, core: 2. Of those that a mesh axis runs over, the one named last changes fastest.
Arguments:
- wavefunction: float32 [2097152], P(('wide', 'narrow')), may hold values from -6 to 6
- propagator: float32 [705432], replicated, may hold values from -2.5 to 3.5, as said below
- gate_orders: int32 [6, 11], replicated, may hold values from 0 to 10, each once within a row
- sector_order: int32 [2048], replicated, may hold values from 0 to 2047, as said below
- bond_level: int32 [20], replicated, may hold values from -3 to 3
Outputs:
- evolved: float32 [2097152], P(('wide', 'narrow'))
Inputs may be any that keep to these rules, and one draw needn't show every extreme that they name: `propagator`: sector blocks for k = 0 .. 11 set bits, each row-major, one after another in increasing k. `sector_order`: a permutation of 0 .. 2047 listing states with fewer set bits first.
All inputs are finite; a program needn't handle non-finite values.
Results may differ from a plain program's by a relative error of at most 0.0001.
Values sent between devices are 32-bit elements; how exact they have to be, the bound alone decides.
A program may use at most 64 MiB of HBM per device.

v0:
```python
import collections
import functools
import math

import jax
import jax.numpy as jnp
import numpy as np
from jax import lax
from jax.experimental import pallas as pl
from jax.experimental.pallas import tpu as pltpu
from jax.sharding import PartitionSpec as P

LB = 16
GS = 11
GATES = 6
ZZ_RATE = 0.06
LANES = 128
ROWS = 512
BF = jnp.bfloat16
F32 = jnp.float32


def up(value, unit):
    return -(-value // unit) * unit


RUN_SIZE = [math.comb(9, s) for s in range(10)]
RUN_PAD = [up(n, 16) for n in RUN_SIZE]
RUN_OFF = [sum(RUN_PAD[:s]) for s in range(10)]
SORTED = sum(RUN_PAD)
SORTED_K = up(SORTED, LANES)
GROUPS = [[0, 1, 2], [3], [4], [5], [6], [7], [8], [9, 10, 11]]
GROUP_SIZE = [256, 256, 384, 512, 512, 384, 256, 256]
GROUP_OFF = [sum(GROUP_SIZE[:i]) for i in range(8)]
TOTAL = sum(GROUP_SIZE)
SECTOR = [math.comb(GS, k) for k in range(GS + 1)]
PROP_OFF = [sum(n * n for n in SECTOR[:k]) for k in range(GS + 1)]
SOURCE_ROWS = 5640
WEIGHT = [0, 1, 1, 2]
J_ROWS = [96, 176, 336, 464, 464, 336, 176, 96]
ORDER = [3, 4, 2, 5, 1, 6, 0, 7]
J_LANES = [128, 256, 384, 512, 512, 384, 256, 128]
A_ROWS = [160, 208, 368, 480, 480, 368, 208, 160]


def layout():
    pieces = []
    sector_row = {}
    for group, sectors in enumerate(GROUPS):
        at = GROUP_OFF[group]
        rows = GROUP_OFF[group]
        for k in sectors:
            sector_row[k] = rows
            rows += up(SECTOR[k], 16)
            for a in range(4):
                s = k - WEIGHT[a]
                if 0 <= s <= 9:
                    pieces.append((s, a, at))
                    at += RUN_PAD[s]
    return pieces, sector_row


PIECES, SECTOR_ROW = layout()


def tables():
    order = -np.ones(SORTED, np.int64)
    for s in range(10):
        rows = [r for r in range(ROWS) if bin(r).count("1") == s]
        order[RUN_OFF[s] : RUN_OFF[s] + len(rows)] = rows
    sort = np.zeros((SORTED, ROWS), np.float32)
    for p in range(SORTED):
        if order[p] >= 0:
            sort[p, order[p]] = 1
    unsort = np.zeros((ROWS, SORTED_K), np.float32)
    unsort[:, :SORTED] = sort.T
    state = -2 * np.ones((2, TOTAL), np.int32)
    for s, a, at in PIECES:
        for i in range(RUN_SIZE[s]):
            r = int(order[RUN_OFF[s] + i])
            state[0, at + i] = r * 4 + a
            state[1, at + i] = (r % 128) + 128 * a + 512 * (r // 128)
    return sort, unsort, state


SORT, UNSORT, STATE = tables()


def dot(a, b):
    return jnp.dot(a, b, preferred_element_type=F32)


def lane_iota(rows):
    return lax.broadcasted_iota(jnp.int32, (rows, LANES), 1)


def halves(x):
    hi = x.astype(BF)
    return hi, (x - hi.astype(F32)).astype(BF)


def unpack_blocks(prop, blocks, outs):
    for t in range(4):
        for group in (0, 7):
            blocks[t, GROUP_OFF[group] : GROUP_OFF[group] + 256, :] = jnp.zeros((256, LANES), F32)
    for k in range(GS + 1):
        n = SECTOR[k]
        if n > 100:
            period = 128 // math.gcd(n, 128)
            group = [i for i, g in enumerate(GROUPS) if g == [k]][0]
            size = GROUP_SIZE[group]
            count, stride = size // period, n * period // 128
        else:
            period, count, stride = n, 1, 1
            size = LANES
        shift_lane = SECTOR_ROW[k] - GROUP_OFF[[k in g for g in GROUPS].index(True)] if n < 100 else 0
        for i in range(period):
            start = PROP_OFF[k] + i * n
            q, r = divmod(start, 128)
            tiles = size // LANES
            lanes = lane_iota(count)
            rolled = []
            for t in range(tiles + (1 if r else 0)):
                if count > 1:
                    v = prop[pl.ds(q + t, count, stride=stride), :]
                else:
                    v = prop[q + t : q + t + 1, :]
                rolled.append(pltpu.roll(v, 128 - r, 1) if r else v)
            for t in range(tiles):
                v = jnp.where(lanes < 128 - r, rolled[t], rolled[t + 1]) if r else rolled[t]
                row = SECTOR_ROW[k] + i
                if count > 1:
                    blocks[t, pl.ds(row, count, stride=period), :] = v
                else:
                    v = jnp.where(lanes < n, v, 0.0)
                    base, within = divmod(shift_lane, 128)
                    if within:
                        v = pltpu.roll(v, within, 1)
                    blocks[base, row : row + 1, :] = v
    for group in range(8):
        rows = slice(GROUP_OFF[group], GROUP_OFF[group] + J_ROWS[group])
        width = J_LANES[group]
        for t in range(width // LANES):
            hi, lo = halves(blocks[t, rows, :])
            outs[group][:, t * LANES : (t + 1) * LANES] = hi
            outs[group][:, width + t * LANES : width + (t + 1) * LANES] = lo


def tile_rows(value, rows):
    return jnp.concatenate([value] * (rows // 16), axis=0)


def equal(column, across, rows, width):
    spread = jnp.broadcast_to(column, (rows, LANES)).astype(jnp.int16)
    spread = jnp.concatenate([spread] * (width // LANES), axis=1)
    return jnp.where(spread == tile_rows(across, rows), jnp.ones((), BF), jnp.zeros((), BF))


def pick_matrix(form, gate, group, refs):
    at, rows, width = GROUP_OFF[group], J_ROWS[group], GROUP_SIZE[group]
    across = refs.state16[16 * form : 16 * form + 16, at : at + width]
    return equal(refs.c_col[at : at + rows, gate : gate + 1], across, rows, width)


def place_matrix(form, gate, group, refs):
    at, rows, width = GROUP_OFF[group], A_ROWS[group], J_LANES[group]
    across = refs.c16[16 * gate : 16 * gate + 16, at : at + width]
    return equal(refs.c_col[at : at + rows, GATES + form : GATES + form + 1], across, rows, width)


def prebuild(form, gate, refs):
    for group in range(8):
        at = GROUP_OFF[group]
        refs.pick[at : at + J_ROWS[group], : GROUP_SIZE[group]] = pick_matrix(form, gate, group, refs)
        refs.place[at : at + A_ROWS[group], : J_LANES[group]] = place_matrix(form, gate, group, refs)


def fetch(refs, group):
    return pltpu.make_async_copy(refs.given[group], refs.blocks[group], refs.block_sem.at[group])


def apply_gate(x, form, gate, refs, built=False):
    xin, yin, sorted_out = refs.xin, refs.yin, refs.sorted_out
    hi, lo = halves(x)
    ordered = dot(refs.sort[...], jnp.concatenate([hi, lo], axis=1))
    oh, ol = ordered[:, :LANES], ordered[:, LANES:]
    lanes = lane_iota(SORTED)
    for a in range(4):
        ra = pltpu.roll(oh, 128 - 32 * a, 1) if a else oh
        rb = pltpu.roll(ol, (160 - 32 * a) % 128, 1) if (160 - 32 * a) % 128 else ol
        mixed = jnp.where(lanes < 32, ra, jnp.where(lanes < 64, rb, 0.0)).astype(BF)
        for s, own, at in PIECES:
            if own == a:
                xin[at : at + RUN_PAD[s], :] = mixed[RUN_OFF[s] : RUN_OFF[s] + RUN_PAD[s], :]
    zbuf, ybuf = refs.zbuf, refs.ybuf
    for group in ORDER:
        at, jr, size = GROUP_OFF[group], J_ROWS[group], GROUP_SIZE[group]
        pick = refs.pick[at : at + jr, :size] if built else pick_matrix(form, gate, group, refs)
        zbuf[at : at + jr, :] = dot(pick, xin[at : at + size, :]).astype(BF)
    for group in ORDER:
        at, jr, jl = GROUP_OFF[group], J_ROWS[group], J_LANES[group]
        if gate == 0:
            fetch(refs, group).wait()
        z = zbuf[at : at + jl, :]
        t = dot(refs.blocks[group][...], jnp.concatenate([z, z], axis=0))
        lane = lane_iota(jr)
        y = jnp.where(lane < 32, t + pltpu.roll(t, 96, 1), t + pltpu.roll(t, 32, 1))
        yh = y.astype(BF).astype(F32)
        y2 = jnp.where(lane < 32, yh, jnp.where(lane < 64, y - yh, 0.0))
        ybuf[at : at + jr, :] = y2.astype(BF)
    for group in ORDER:
        at, jl, ar = GROUP_OFF[group], J_LANES[group], A_ROWS[group]
        place = refs.place[at : at + ar, :jl] if built else place_matrix(form, gate, group, refs)
        yin[at : at + ar, :] = dot(place, ybuf[at : at + jl, :])
    for s in range(10):
        lanes = lane_iota(RUN_PAD[s])
        hi = lo = None
        for run, a, at in PIECES:
            if run == s:
                w = yin[at : at + RUN_PAD[s], :]
                h = pltpu.roll(w, 32 * a, 1) if a else w
                l = pltpu.roll(w, (32 * a + 96) % 128, 1) if a != 1 else w
                own = (lanes >= 32 * a) & (lanes < 32 * a + 32)
                hi = h if hi is None else jnp.where(own, h, hi)
                lo = l if lo is None else jnp.where(own, l, lo)
        sorted_out[RUN_OFF[s] : RUN_OFF[s] + RUN_PAD[s], :] = jnp.concatenate([hi, lo], axis=1).astype(BF)
    result = dot(refs.unsort[...], sorted_out[...])
    return result[:, :LANES] + result[:, LANES:]


def to_low(x_ref):
    parts = []
    for h1 in range(4):
        stack = [x_ref[pl.ds(h1 * 4 + a, 32, stride=16), :] for a in range(4)]
        parts.append(jnp.transpose(jnp.concatenate(stack, axis=0)))
    return jnp.concatenate(parts, axis=0)


def from_low(x, x_ref):
    for h1 in range(4):
        turned = jnp.transpose(x[h1 * 128 : (h1 + 1) * 128, :])
        for a in range(4):
            x_ref[pl.ds(h1 * 4 + a, 32, stride=16), :] = turned[32 * a : 32 * a + 32, :]


def spin(index, position):
    return (1 - 2 * (jnp.right_shift(index, position) & 1)).astype(F32)


def phase(high, level):
    lane = lax.broadcasted_iota(jnp.int32, (1, LANES), 1)
    row = lax.broadcasted_iota(jnp.int32, (ROWS, 1), 0)
    lv = [level[s].astype(F32) for s in range(level.shape[0])]
    lane_z = [spin(lane, s) for s in range(7)]
    row_z = [spin(row, s) for s in range(9)]
    lane_e = sum(lv[s] * lane_z[s] * lane_z[s + 1] for s in range(6))
    row_e = sum(lv[7 + s] * row_z[s] * row_z[s + 1] for s in range(8))
    row_e = row_e + row_z[8] * (lv[LB - 1] * spin(high, 0))
    for s in range(level.shape[0] - LB):
        row_e = row_e + lv[LB + s] * spin(high, s) * spin(high, s + 1)
    energy = lane_e + row_e + (lv[6] * row_z[0]) * lane_z[6]
    return jnp.exp(-ZZ_RATE * energy)


def padded_states(sectors):
    lane = lane_iota(1)
    tiles = []
    for tile in range(TOTAL // LANES):
        value = jnp.full((1, LANES), -1, jnp.int32)
        first = 0
        for k in range(GS + 1):
            n, begin = SECTOR[k], SECTOR_ROW[k] - tile * LANES
            low, high = max(begin, 0), min(begin + n, LANES)
            if low < high:
                q, r = divmod(first - begin, LANES)
                for step in (0, 1):
                    a, b = (low, min(high, LANES - r)) if step == 0 else (max(low, LANES - r), high)
                    if a < b:
                        row = sectors[q + step : q + step + 1, :]
                        row = pltpu.roll(row, LANES - r, 1) if r else row
                        value = jnp.where((lane >= a) & (lane < b), row, value)
            first += n
        tiles.append(value)
    return jnp.concatenate(tiles, axis=1)


def index_maps(orders, sectors, state, refs):
    states = padded_states(sectors)
    maps = []
    for g in range(GATES):
        c = jnp.zeros(states.shape, jnp.int32)
        for t in range(GS):
            c = c + jnp.left_shift(jnp.right_shift(states, t) & 1, orders[g, t])
        c = jnp.where(states < 0, -1, c)
        refs.c16[16 * g : 16 * g + 16, :] = jnp.broadcast_to(c, (16, TOTAL)).astype(jnp.int16)
        maps.append(c)
    for form in range(2):
        own = state[form : form + 1, :]
        refs.state16[16 * form : 16 * form + 16, :] = jnp.broadcast_to(own, (16, TOTAL)).astype(jnp.int16)
        maps.append(own)
    refs.c_col[...] = jnp.transpose(jnp.concatenate(maps, axis=0))


class Exchange:
    def __init__(self, wide, narrow, source, target, send_sem, recv_sem):
        self.wide, self.count = wide, wide * narrow
        self.me = lax.axis_index("narrow") * wide + lax.axis_index("wide")
        self.source, self.target, self.sems = source, target, (send_sem, recv_sem)

    def device(self, t):
        return {"wide": lax.rem(t, self.wide), "narrow": t // self.wide}

    def greet(self):
        barrier = pltpu.get_barrier_semaphore()

        @pl.loop(1, self.count)
        def _(off):
            t = lax.rem(self.me + off, self.count)
            pl.semaphore_signal(barrier, inc=1, device_id=self.device(t), device_id_type=MESH)

    def greeted(self):
        pl.semaphore_wait(pltpu.get_barrier_semaphore(), self.count - 1)

    def start(self):
        @pl.loop(1, self.count)
        def _(off):
            t = lax.rem(self.me + off, self.count)
            pltpu.make_async_remote_copy(
                src_ref=self.source.at[t],
                dst_ref=self.target.at[self.me],
                send_sem=self.sems[0],
                recv_sem=self.sems[1],
                device_id=self.device(t),
                device_id_type=MESH,
            ).start()

        self.target[pl.ds(self.me, 1)] = self.source[pl.ds(self.me, 1)]

    def wait(self):
        rest = pl.ds(0, self.count - 1)
        both = pltpu.make_async_remote_copy(
            src_ref=self.source.at[rest],
            dst_ref=self.target.at[rest],
            send_sem=self.sems[0],
            recv_sem=self.sems[1],
            device_id=self.device(lax.rem(self.me + 1, self.count)),
            device_id_type=MESH,
        )
        both.wait_send()
        both.wait_recv()


def unpack_kernel(prop, *rest):
    unpack_blocks(prop, rest[8], rest[:8])


Refs = collections.namedtuple(
    "Refs",
    ["sort", "unsort", "given", "blocks", "block_sem", "state16", "c16", "c_col"]
    + ["xin", "zbuf", "ybuf", "yin", "sorted_out", "pick", "place"],
)


def gates_kernel(wide, narrow, level, orders, wave, sectors, state, sort, unsort, *rest):
    given, out, blocks = rest[:8], rest[8], rest[9:17]
    state16, c16, c_col, xin, zbuf, ybuf, yin, sorted_out, pick, place, x, sent, landed = rest[17:30]
    block_sem, send_sem, recv_sem = rest[30:]
    refs = Refs(
        sort, unsort, given, blocks, block_sem, state16, c16, c_col,
        xin, zbuf, ybuf, yin, sorted_out, pick, place,
    )
    for group in ORDER:
        fetch(refs, group).start()
    there = Exchange(wide, narrow, sent.at[0], landed.at[0], send_sem.at[0], recv_sem.at[0])
    back = Exchange(wide, narrow, sent.at[1], landed.at[1], send_sem.at[1], recv_sem.at[1])
    shape = sent.shape[1:]
    there.greet()
    for zeroed in (xin, zbuf, ybuf):
        zeroed[...] = jnp.zeros(zeroed.shape, BF)
    sorted_out[...] = jnp.zeros(sorted_out.shape, BF)
    index_maps(orders, sectors, state, refs)
    high = lax.axis_index("wide") * narrow + lax.axis_index("narrow")
    x[...] = apply_gate(wave[...] * phase(high, level), 0, 0, refs)
    from_low(apply_gate(to_low(x), 1, 1, refs), x)
    sent[0] = x[...].reshape(shape)
    there.greeted()
    there.start()
    prebuild(0, 2, refs)
    there.wait()
    sent[1] = apply_gate(landed[0].reshape(ROWS, LANES), 0, 2, refs, True).reshape(shape)
    back.start()
    prebuild(1, 3, refs)
    back.wait()
    x[...] = landed[1].reshape(ROWS, LANES)
    from_low(apply_gate(to_low(x), 1, 3, refs, True), x)
    x[...] = apply_gate(x[...], 0, 4, refs)
    from_low(apply_gate(to_low(x), 1, 5, refs), out)


SMEM = pl.BlockSpec(memory_space=pltpu.SMEM)
VMEM = pl.BlockSpec(memory_space=pltpu.VMEM)
MESH = pl.DeviceIdType.MESH


def shards(wavefunction, propagator, gate_orders, sector_order, bond_level):
    wide, narrow = lax.axis_size("wide"), lax.axis_size("narrow")
    count = wide * narrow
    source = jnp.pad(propagator, (0, SOURCE_ROWS * LANES - propagator.shape[0])).reshape(SOURCE_ROWS, LANES)
    shapes = [(J_ROWS[g], 2 * J_LANES[g]) for g in range(8)]
    blocks = pl.pallas_call(
        unpack_kernel,
        out_shape=[jax.ShapeDtypeStruct(shape, BF) for shape in shapes],
        in_specs=[VMEM],
        out_specs=[VMEM] * 8,
        scratch_shapes=[pltpu.VMEM((4, TOTAL, LANES), F32)],
        compiler_params=pltpu.CompilerParams(vmem_limit_bytes=32 * 2**20),
        name="unpack_blocks",
    )(source)
    x = pl.pallas_call(
        functools.partial(gates_kernel, wide, narrow),
        out_shape=jax.ShapeDtypeStruct((ROWS, LANES), F32),
        in_specs=[SMEM, SMEM] + [VMEM] * 5 + [pl.BlockSpec(memory_space=pl.ANY)] * 8,
        out_specs=VMEM,
        scratch_shapes=[pltpu.VMEM(shape, BF) for shape in shapes]
        + [
            pltpu.VMEM((32, TOTAL), jnp.int16),
            pltpu.VMEM((16 * GATES, TOTAL), jnp.int16),
            pltpu.VMEM((TOTAL, 8), jnp.int32),
            pltpu.VMEM((TOTAL, LANES), BF),
            pltpu.VMEM((TOTAL, LANES), BF),
            pltpu.VMEM((TOTAL, LANES), BF),
            pltpu.VMEM((TOTAL, LANES), F32),
            pltpu.VMEM((SORTED_K, 2 * LANES), BF),
            pltpu.VMEM((TOTAL, 512), BF),
            pltpu.VMEM((TOTAL, 512), BF),
            pltpu.VMEM((ROWS, LANES), F32),
            pltpu.VMEM((2, count, ROWS // count, LANES), F32),
            pltpu.VMEM((2, count, ROWS // count, LANES), F32),
            pltpu.SemaphoreType.DMA((8,)),
            pltpu.SemaphoreType.DMA((2,)),
            pltpu.SemaphoreType.DMA((2,)),
        ],
        compiler_params=pltpu.CompilerParams(
            vmem_limit_bytes=44 * 2**20, collective_id=0, has_side_effects=True
        ),
        name="six_gates",
    )(
        bond_level,
        gate_orders,
        wavefunction.reshape(ROWS, LANES),
        sector_order.reshape(-1, LANES),
        jnp.asarray(STATE),
        jnp.asarray(SORT, BF),
        jnp.asarray(UNSORT, BF),
        *blocks,
    )
    return x.reshape(-1)


def solution(mesh):
    in_specs = (P(("wide", "narrow")), P(), P(), P(), P())
    out_specs = P(("wide", "narrow"))
    return jax.shard_map(shards, mesh=mesh, in_specs=in_specs, out_specs=out_specs, check_vma=False)
```

profile of v0, /device:TPU:0, one launch (start us, length us, event | category | flops | bytes accessed | tf_op | source)
XLA Modules:
  0.0 55.6 jit_solution(7045502295676035249)
XLA Ops:
  0.0 0.0 copy-start
  0.0 0.0 copy-start.1
  0.0 0.0 copy-start.2
  0.0 0.0 copy-start.3
  0.0 0.0 copy-start.4
  0.0 0.0 copy-start.5
  0.0 0.0 copy-start.6
  0.0 2.1 %pad_bitcast_fusion.prop = f32[5640,128]{1,0:T(8,128)S(1)} fusion(f32[705432]{0:T(1024)} %param.9), kind=kLoop, calls=%fused_computation | loop fusion | bytes 5709408 | tf_op jit(solution)/shard_map/reshape | solution.py:408
  2.1 7.5 %unpack_blocks.1 = (bf16[96,256]{1,0:T(8,128)(2,1)S(1)}, bf16[176,512]{1,0:T(8,128)(2,1)S(1)}, bf16[336,768]{1,0:T(8,128)(2,1)S(1)}, bf16[464,1024]{1,0:T(8,128)...) custom-call(f32[5640,128]{1,0:T(8,128)S(1)} %pad_bitcast_fusion.prop), custom_call_target="tpu_custom_call" | custom-call | tf_op jit(solution)/shard_map/unpack_blocks/pallas_call | solution.py:410
  9.6 0.0 copy-done
  9.6 0.0 copy-done.1
  9.6 0.0 copy-done.2
  9.7 0.0 copy-done.3
  9.7 0.0 copy-done.4
  9.7 0.0 copy-done.5
  9.7 0.0 copy-done.6
  9.7 45.2 %six_gates.1 = f32[512,128]{1,0:T(8,128)S(1)} custom-call(s32[20]{0:T(128)S(1)} %copy-done.6, s32[6,11]{1,0:T(8,128)S(1)} %copy-done.5, f32[512,128]{1,0:T(8,128)S(1)} %bitcast.6, s32[16,128]{1,0:T(8,128)S(1)} %bitcast.7, s32[2,2816]{1,0:T(2,128)S(1)} %copy-done.3, bf16[608,512]{1,0:T(8,128)(2,1)S(1)} %copy-done.1, bf16[512,640]{1,0:T(8,128)(2,1)S(1)} %copy-done, ...), custom_call_target="tpu_custom_call" | custom-call | tf_op jit(solution)/shard_map/six_gates/pallas_call | solution.py:419
  54.9 0.7 %copy.10 = f32[65536]{0:T(1024)} copy(f32[65536]{0:T(1024)S(1)} %bitcast.5) | data formatting | bytes 524288
Async XLA Ops:
  0.0 9.6 %copy-start = (bf16[512,640]{1,0:T(8,128)(2,1)S(1)}, bf16[512,640]{1,0:T(8,128)(2,1)}, u32[]{:S(2)}) copy-start(bf16[512,640]{1,0:T(8,128)(2,1)} %constant.11.clone.unsort) | copy-start | bytes 1966084
  0.0 9.6 %copy-start.1 = (bf16[608,512]{1,0:T(8,128)(2,1)S(1)}, bf16[608,512]{1,0:T(8,128)(2,1)}, u32[]{:S(2)}) copy-start(bf16[608,512]{1,0:T(8,128)(2,1)} %constant.10.clone.sort) | copy-start | bytes 1867780
  0.0 9.6 %copy-start.2 = (f32[65536]{0:T(1024)S(1)}, f32[65536]{0:T(1024)}, u32[]{:S(2)}) copy-start(f32[65536]{0:T(1024)} %param.8) | copy-start | bytes 786436
  0.0 9.6 %copy-start.3 = (s32[2,2816]{1,0:T(2,128)S(1)}, s32[2,2816]{1,0:T(2,128)}, u32[]{:S(2)}) copy-start(s32[2,2816]{1,0:T(2,128)} %constant.9.clone.state) | copy-start | bytes 67588
  0.0 9.7 %copy-start.4 = (s32[2048]{0:T(1024)S(1)}, s32[2048]{0:T(1024)}, u32[]{:S(2)}) copy-start(s32[2048]{0:T(1024)} %param.11) | copy-start | bytes 24580
  0.0 9.7 %copy-start.5 = (s32[6,11]{1,0:T(8,128)S(1)}, s32[6,11]{1,0:T(8,128)}, u32[]{:S(2)}) copy-start(s32[6,11]{1,0:T(8,128)} %orders.1) | copy-start | bytes 796
  0.0 9.7 %copy-start.6 = (s32[20]{0:T(128)S(1)}, s32[20]{0:T(128)}, u32[]{:S(2)}) copy-start(s32[20]{0:T(128)} %level.1) | copy-start | bytes 244
where the time goes:
time: 55.8 us; the launch traced here: 55.6 us
  Pallas kernels  52.7 us (94%)
  local copies, waits for them, and re-layouts  2.84 us (5%)
    pallas_call x1, Pallas kernels, shards(): pl.pallas_call(functools.partial(gates_kernel, wide, narrow), out_shape=j...  45.2 us
    pallas_call x1, Pallas kernels, shards(): pl.pallas_call(unpack_kernel, out_shape=[jax.ShapeDtypeStruct(shape, BF)...  7.49 us
    reshape x1, local copies, waits for them, and re-layouts, shards(): jnp.pad(propagator, (0, SOURCE_ROWS * LANES - propagator.shape[0]))  2.1 us

commit v1 on v0

--- a/solution.py
+++ b/solution.py
@@ -171,8 +171,8 @@
 def prebuild(form, gate, refs):
     for group in range(8):
         at = GROUP_OFF[group]
-        refs.pick[at : at + J_ROWS[group], : GROUP_SIZE[group]] = pick_matrix(form, gate, group, refs)
-        refs.place[at : at + A_ROWS[group], : J_LANES[group]] = place_matrix(form, gate, group, refs)
+        refs.pick[gate - 2, at : at + J_ROWS[group], : GROUP_SIZE[group]] = pick_matrix(form, gate, group, refs)
+        refs.place[gate - 2, at : at + A_ROWS[group], : J_LANES[group]] = place_matrix(form, gate, group, refs)
 
 
 def fetch(refs, group):
@@ -195,7 +195,7 @@
     zbuf, ybuf = refs.zbuf, refs.ybuf
     for group in ORDER:
         at, jr, size = GROUP_OFF[group], J_ROWS[group], GROUP_SIZE[group]
-        pick = refs.pick[at : at + jr, :size] if built else pick_matrix(form, gate, group, refs)
+        pick = refs.pick[gate - 2, at : at + jr, :size] if built else pick_matrix(form, gate, group, refs)
         zbuf[at : at + jr, :] = dot(pick, xin[at : at + size, :]).astype(BF)
     for group in ORDER:
         at, jr, jl = GROUP_OFF[group], J_ROWS[group], J_LANES[group]
@@ -210,7 +210,7 @@
         ybuf[at : at + jr, :] = y2.astype(BF)
     for group in ORDER:
         at, jl, ar = GROUP_OFF[group], J_LANES[group], A_ROWS[group]
-        place = refs.place[at : at + ar, :jl] if built else place_matrix(form, gate, group, refs)
+        place = refs.place[gate - 2, at : at + ar, :jl] if built else place_matrix(form, gate, group, refs)
         yin[at : at + ar, :] = dot(place, ybuf[at : at + jl, :])
     for s in range(10):
         lanes = lane_iota(RUN_PAD[s])
@@ -386,15 +386,17 @@
     there.greeted()
     there.start()
     prebuild(0, 2, refs)
+    prebuild(0, 4, refs)
     there.wait()
     sent[1] = apply_gate(landed[0].reshape(ROWS, LANES), 0, 2, refs, True).reshape(shape)
     back.start()
     prebuild(1, 3, refs)
+    prebuild(1, 5, refs)
     back.wait()
     x[...] = landed[1].reshape(ROWS, LANES)
     from_low(apply_gate(to_low(x), 1, 3, refs, True), x)
-    x[...] = apply_gate(x[...], 0, 4, refs)
-    from_low(apply_gate(to_low(x), 1, 5, refs), out)
+    x[...] = apply_gate(x[...], 0, 4, refs, True)
+    from_low(apply_gate(to_low(x), 1, 5, refs, True), out)
 
 
 SMEM = pl.BlockSpec(memory_space=pltpu.SMEM)
@@ -431,8 +433,8 @@
             pltpu.VMEM((TOTAL, LANES), BF),
             pltpu.VMEM((TOTAL, LANES), F32),
             pltpu.VMEM((SORTED_K, 2 * LANES), BF),
-            pltpu.VMEM((TOTAL, 512), BF),
-            pltpu.VMEM((TOTAL, 512), BF),
+            pltpu.VMEM((GATES - 2, TOTAL, 512), BF),
+            pltpu.VMEM((GATES - 2, TOTAL, 512), BF),
             pltpu.VMEM((ROWS, LANES), F32),
             pltpu.VMEM((2, count, ROWS // count, LANES), F32),
             pltpu.VMEM((2, count, ROWS // count, LANES), F32),

time: 55.8 us -> 55.6 us (level)
  no operation moved by 1% of the time
where the time goes in v1:
time: 55.6 us; the launch traced here: 55.4 us
  Pallas kernels  52.5 us (94%)
  local copies, waits for them, and re-layouts  2.84 us (5%)
    pallas_call x1, Pallas kernels, shards(): pl.pallas_call(functools.partial(gates_kernel, wide, narrow), out_shape=j...  45 us
    pallas_call x1, Pallas kernels, shards(): pl.pallas_call(unpack_kernel, out_shape=[jax.ShapeDtypeStruct(shape, BF)...  7.49 us
    reshape x1, local copies, waits for them, and re-layouts, shards(): jnp.pad(propagator, (0, SOURCE_ROWS * LANES - propagator.shape[0]))  2.1 us

profile of v1, /device:TPU:0, one launch (start us, length us, event | category | flops | bytes accessed | tf_op | source)
XLA Modules:
  0.0 55.4 jit_solution(14499572436225963036)
XLA Ops:
  0.0 0.0 copy-start
  0.0 0.0 copy-start.1
  0.0 0.0 copy-start.2
  0.0 0.0 copy-start.3
  0.0 0.0 copy-start.4
  0.0 0.0 copy-start.5
  0.0 0.0 copy-start.6
  0.0 2.1 %pad_bitcast_fusion.prop = f32[5640,128]{1,0:T(8,128)S(1)} fusion(f32[705432]{0:T(1024)} %param.9), kind=kLoop, calls=%fused_computation | loop fusion | bytes 5709408 | tf_op jit(solution)/shard_map/reshape | solution.py:410
  2.1 7.5 %unpack_blocks.1 = (bf16[96,256]{1,0:T(8,128)(2,1)S(1)}, bf16[176,512]{1,0:T(8,128)(2,1)S(1)}, bf16[336,768]{1,0:T(8,128)(2,1)S(1)}, bf16[464,1024]{1,0:T(8,128)...) custom-call(f32[5640,128]{1,0:T(8,128)S(1)} %pad_bitcast_fusion.prop), custom_call_target="tpu_custom_call" | custom-call | tf_op jit(solution)/shard_map/unpack_blocks/pallas_call | solution.py:412
  9.6 0.0 copy-done
  9.6 0.0 copy-done.1
  9.6 0.0 copy-done.2
  9.7 0.0 copy-done.3
  9.7 0.0 copy-done.4
  9.7 0.0 copy-done.5
  9.7 0.0 copy-done.6
  9.7 45.0 %six_gates.1 = f32[512,128]{1,0:T(8,128)S(1)} custom-call(s32[20]{0:T(128)S(1)} %copy-done.6, s32[6,11]{1,0:T(8,128)S(1)} %copy-done.5, f32[512,128]{1,0:T(8,128)S(1)} %bitcast.6, s32[16,128]{1,0:T(8,128)S(1)} %bitcast.7, s32[2,2816]{1,0:T(2,128)S(1)} %copy-done.3, bf16[608,512]{1,0:T(8,128)(2,1)S(1)} %copy-done.1, bf16[512,640]{1,0:T(8,128)(2,1)S(1)} %copy-done, ...), custom_call_target="tpu_custom_call" | custom-call | tf_op jit(solution)/shard_map/six_gates/pallas_call | solution.py:421
  54.7 0.7 %copy.10 = f32[65536]{0:T(1024)} copy(f32[65536]{0:T(1024)S(1)} %bitcast.5) | data formatting | bytes 524288
Async XLA Ops:
  0.0 9.6 %copy-start = (bf16[512,640]{1,0:T(8,128)(2,1)S(1)}, bf16[512,640]{1,0:T(8,128)(2,1)}, u32[]{:S(2)}) copy-start(bf16[512,640]{1,0:T(8,128)(2,1)} %constant.11.clone.unsort) | copy-start | bytes 1966084
  0.0 9.6 %copy-start.1 = (bf16[608,512]{1,0:T(8,128)(2,1)S(1)}, bf16[608,512]{1,0:T(8,128)(2,1)}, u32[]{:S(2)}) copy-start(bf16[608,512]{1,0:T(8,128)(2,1)} %constant.10.clone.sort) | copy-start | bytes 1867780
  0.0 9.6 %copy-start.2 = (f32[65536]{0:T(1024)S(1)}, f32[65536]{0:T(1024)}, u32[]{:S(2)}) copy-start(f32[65536]{0:T(1024)} %param.8) | copy-start | bytes 786436
  0.0 9.6 %copy-start.3 = (s32[2,2816]{1,0:T(2,128)S(1)}, s32[2,2816]{1,0:T(2,128)}, u32[]{:S(2)}) copy-start(s32[2,2816]{1,0:T(2,128)} %constant.9.clone.state) | copy-start | bytes 67588
  0.0 9.7 %copy-start.4 = (s32[2048]{0:T(1024)S(1)}, s32[2048]{0:T(1024)}, u32[]{:S(2)}) copy-start(s32[2048]{0:T(1024)} %param.11) | copy-start | bytes 24580
  0.0 9.7 %copy-start.5 = (s32[6,11]{1,0:T(8,128)S(1)}, s32[6,11]{1,0:T(8,128)}, u32[]{:S(2)}) copy-start(s32[6,11]{1,0:T(8,128)} %orders.1) | copy-start | bytes 796
  0.0 9.7 %copy-start.6 = (s32[20]{0:T(128)S(1)}, s32[20]{0:T(128)}, u32[]{:S(2)}) copy-start(s32[20]{0:T(128)} %level.1) | copy-start | bytes 244
